TPU v7x, 32 devices: a whole 2x2x4 slice. The times are simulated.
32 devices in a mesh: circ: 8 (over z, core), span: 4 (over y, x).
Axes of the slice: x: 2, y: 2, z: 4, core: 2. Of those that a mesh axis runs over, the one named last changes fastest.
Arguments:
- adjoint_rotor: float32 [6, 8, 4, 2048], P(None, 'span', None, 'circ'), may hold values from -6 to 6
- adjoint_stator: float32 [6, 8, 4, 2048], P(None, 'span', None, 'circ'), may hold values from -6 to 6
- jac_diag_rotor: float32 [6, 8, 4, 2048], P(None, 'span', None, 'circ'), may hold values from 2 to 4
- jac_diag_stator: float32 [6, 8, 4, 2048], P(None, 'span', None, 'circ'), may hold values from 2 to 4
- jac_off_rotor: bfloat16 [6, 6, 8, 4, 2048], P(None, None, 'span', None, 'circ'), may hold values from -1 to 1
- jac_off_stator: bfloat16 [6, 6, 8, 4, 2048], P(None, None, 'span', None, 'circ'), may hold values from -1 to 1
- source_rotor: float32 [6, 8, 4, 2048], P(None, 'span', None, 'circ'), may hold values from -6 to 6
- source_stator: float32 [6, 8, 4, 2048], P(None, 'span', None, 'circ'), may hold values from -6 to 6
- rotor_state: bfloat16 [6, 8, 2048], P(None, 'span', 'circ'), may hold values from -6 to 6
- margin_block: int32 [8, 16, 4], P('span'), may hold values from 0 to 15, as said below
- face_count: int32 [8, 16], P('span'), may hold values from 1 to 4
- margin_weight: float32 [8, 16, 4, 128], P('span'), may hold values from 0.2 to 1
Outputs:
- rotor_adjoint: float32 [6, 8, 4, 2048], P(None, 'span', None, 'circ')
- stator_adjoint: float32 [6, 8, 4, 2048], P(None, 'span', None, 'circ')
Inputs may be any that keep to these rules, and one draw needn't show every extreme that they name: `margin_block`: entry k of the list of stator block b in spanwise row s is rotor block (b + o + 2 * 2 * s + 1 + j + k) mod 16, with one o for the whole array and j from 0 to 2 for each block of each row.
All inputs are finite; a program needn't handle non-finite values.
Results may differ from a plain program's by a relative error of at most 0.00055.
Values may be sent and summed in bfloat16 or wider, within the bound.
No kernel may reach another device: no remote copies, remote signals or barrier semaphores. Data moves between devices by JAX's collectives and lax.ppermute only.
A program may use at most 64 MiB of HBM per device.

v0:
```python
import jax
import jax.numpy as jnp
from jax import lax
from jax.sharding import PartitionSpec as P

STEPS = 2


step_size = 0.1
coupling = 0.2
highest = lax.Precision.HIGHEST


def extended(x, sides, width):
    for axis, dim in sides:
        size, length = (lax.axis_size(axis), x.shape[dim])
        up = [(i, (i + 1) % size) for i in range(size)]
        down = [(j, i) for i, j in up]
        last = lax.slice_in_dim(x, length - width, length, axis=dim)
        first = lax.slice_in_dim(x, 0, width, axis=dim)
        before = lax.ppermute(last, axis, up)
        after = lax.ppermute(first, axis, down)
        x = jnp.concatenate([before, x, after], axis=dim)
    return x


def interface_flux(primal, adjoint):
    speeds = jnp.sqrt(1.0 + primal * primal)
    projection = jnp.sum(primal * adjoint, axis=0) / (6.0 + jnp.sum(primal * primal, axis=0))
    return speeds * adjoint + 0.5 * primal * projection[None]


def jacobian_apply(jac_diag, jac_off, adjoint):
    applied = jac_diag * adjoint
    for source_var in range(adjoint.shape[0]):
        applied = applied + jac_off[source_var].astype(jnp.float32) * adjoint[source_var][None]
    return applied


def per_device(
    adjoint_rotor,
    adjoint_stator,
    jac_diag_rotor,
    jac_diag_stator,
    jac_off_rotor,
    jac_off_stator,
    source_rotor,
    source_stator,
    rotor_state,
    margin_block,
    face_count,
    margin_weight,
):
    var_count = adjoint_rotor.shape[0]
    span_rows = adjoint_rotor.shape[1]
    layer_count = adjoint_rotor.shape[2]
    cell_count = adjoint_rotor.shape[3]
    entry_total = margin_weight.shape[2]
    block_width = margin_weight.shape[3]
    own_blocks = cell_count // block_width
    circ_at = lax.axis_index("circ")
    first_block = circ_at * own_blocks
    span_at = lax.axis_index("span")
    span_total = lax.axis_size("span")
    live_mask = (
        jnp.arange(entry_total, dtype=jnp.int32)[None, None, :] < face_count[:, :, None]
    ).astype(jnp.float32)
    weights_live = margin_weight * live_mask[:, :, :, None]
    own_ids = lax.dynamic_slice_in_dim(margin_block, first_block, own_blocks, 1)
    own_weights = lax.dynamic_slice_in_dim(weights_live, first_block, own_blocks, 1)
    portion = lax.all_gather(rotor_state, "circ", axis=2, tiled=True)
    row_count = portion.shape[2] // block_width
    blocks = portion.reshape(var_count, span_rows, row_count, block_width).astype(jnp.float32)
    pick_one_hot = (
        own_ids[:, :, :, None] == jnp.arange(row_count, dtype=jnp.int32)[None, None, None, :]
    ).astype(jnp.float32)
    pick_mixing = jnp.einsum("sbkj,sbkc->sbjc", pick_one_hot, own_weights, precision=highest)
    stator_primal = jnp.einsum("sbjc,vsjc->vsbc", pick_mixing, blocks, precision=highest).reshape(
        var_count, span_rows, cell_count
    )
    low_keep = jnp.where(span_at == 0, 0.0, 1.0).astype(jnp.float32)
    high_keep = jnp.where(span_at == span_total - 1, 0.0, 1.0).astype(jnp.float32)
    below_mask = jnp.ones((span_rows,), jnp.float32).at[0].set(low_keep)[None, None, :, None, None]
    above_mask = (
        jnp.ones((span_rows,), jnp.float32)
        .at[span_rows - 1]
        .set(high_keep)[None, None, :, None, None]
    )
    rotor_adj, stator_adj = (adjoint_rotor, adjoint_stator)
    for sweep in range(STEPS):
        stacked = jnp.stack((rotor_adj, stator_adj))
        padded = extended(stacked.astype(jnp.bfloat16), (("circ", 4), ("span", 2)), 1).astype(
            stacked.dtype
        )
        inner = padded[:, :, 1:-1, :, :]
        beside_all = inner[:, :, :, :, 2:] + inner[:, :, :, :, :-2]
        layer_pad = jnp.pad(stacked, ((0, 0), (0, 0), (0, 0), (1, 1), (0, 0)))
        beside_all = beside_all + layer_pad[:, :, :, 2:] + layer_pad[:, :, :, :-2]
        beside_all = (
            beside_all
            + padded[:, :, :-2, :, 1:-1] * below_mask
            + padded[:, :, 2:, :, 1:-1] * above_mask
        )
        face_flux = interface_flux(stator_primal, stator_adj[:, :, 0, :])
        flux_wire = face_flux.astype(jnp.bfloat16)
        flux_blocks = flux_wire.astype(jnp.float32).reshape(
            var_count, span_rows, own_blocks, block_width
        )
        one_hot = (
            own_ids[:, :, :, None]
            == jnp.arange(own_blocks * lax.axis_size("circ"), dtype=jnp.int32)[None, None, None, :]
        ).astype(jnp.float32)
        mixing = jnp.einsum("sbkj,sbkc->sbjc", one_hot, own_weights, precision=highest)
        pulled_blocks = lax.psum_scatter(
            jnp.einsum("sbjc,vsbc->jvsc", mixing, flux_blocks, precision=highest),
            "circ",
            scatter_dimension=0,
            tiled=True,
        )
        pulled = jnp.transpose(pulled_blocks, (1, 2, 0, 3)).reshape(
            var_count, span_rows, cell_count
        )
        rotor_res = (
            jacobian_apply(jac_diag_rotor, jac_off_rotor, rotor_adj)
            - coupling * beside_all[0]
            - source_rotor
        )
        rotor_res = rotor_res.at[:, :, layer_count - 1, :].add(-pulled)
        stator_res = (
            jacobian_apply(jac_diag_stator, jac_off_stator, stator_adj)
            - coupling * beside_all[1]
            - source_stator
        )
        stator_res = stator_res.at[:, :, 0, :].add(face_flux)
        rotor_adj = rotor_adj - step_size * rotor_res
        stator_adj = stator_adj - step_size * stator_res
    return (rotor_adj, stator_adj)


def solution(mesh):
    placed = (
        P(None, "span", None, "circ"),
        P(None, "span", None, "circ"),
        P(None, "span", None, "circ"),
        P(None, "span", None, "circ"),
        P(None, None, "span", None, "circ"),
        P(None, None, "span", None, "circ"),
        P(None, "span", None, "circ"),
        P(None, "span", None, "circ"),
        P(None, "span", "circ"),
        P("span", None, None),
        P("span", None),
        P("span", None, None, None),
    )
    return jax.shard_map(
        per_device,
        mesh=mesh,
        in_specs=placed,
        out_specs=(P(None, "span", None, "circ"), P(None, "span", None, "circ")),
        check_vma=False,
    )
```

profile of v0, /device:TPU:0, one launch (start us, length us, event | category | flops | bytes accessed | tf_op | source)
XLA Modules:
  0.0 116.4 jit_solution(17396251983541591181)
XLA Ops:
  7.2 0.9 copy_bitcast_fusion
  8.3 0.5 collective-permute-start
  8.8 4.1 %collective-permute-start.1 = (bf16[2,6,2,4,1]{4,2,1,3,0:T(2,128)(2,1)S(1)}, bf16[2,6,2,4,1]{4,2,1,3,0:T(2,128)(2,1)S(1)}, u32[]{:S(2)}, u32[]{:S(2)}) collective-permute-start(bf16[2,6,2,4,1]{4,2,1,3,0:T(2,128)(2,1)S(1)} %get-tuple-element.129), channel_id=1, source_target_pairs={{4,0},{8,4},{12,8},{16,12},{20,16},{24,20},{28,24},{0,28},{5,1},{9... | collective-permute-start | bytes 584 | tf_op jit(solution)/shard_map/ppermute | solution.py:22
  13.0 0.7 copy-done.10
  13.9 1.0 fusion.51
  14.9 0.2 copy.148
  15.1 0.5 copy-done.9
  15.6 10.8 %all_gather.3 = bf16[6,2,2048]{2,1,0:T(2,128)(2,1)S(1)} all-gather(bf16[6,2,256]{2,1,0:T(2,128)(2,1)S(1)} %copy-done.9), channel_id=1, replica_groups=mesh['circ'=8,'span'=4] {'circ'}, dimensions={2}, use_global_device_ids=true | all-gather | bytes 55296 | tf_op jit(solution)/shard_map/all_gather | solution.py:71
  26.5 0.3 copy.149
  26.8 0.6 copy-done.8
  27.4 1.0 fusion.63
  28.4 0.2 pad_maximum_fusion.2
  28.6 0.1 fusion.60
  28.8 1.5 %collective-permute-start.2 = (bf16[2,6,1,4,258]{4,2,1,3,0:T(2,128)(2,1)S(1)}, bf16[2,6,1,4,258]{4,2,1,3,0:T(2,128)(2,1)S(1)}, u32[]{:S(2)}, u32[]{:S(2)}) collective-permute-start(bf16[2,6,1,4,258]{4,2,1,3,0:T(2,128)(2,1)S(1)} %get-tuple-element.98), channel_id=1, source_target_pairs={{0,1},{1,2},{2,3},{3,0},{4,5},{5,6},{6,7},{7,4},{8,9},{9,10},{10,1... | collective-permute-start | bytes 74312 | tf_op jit(solution)/shard_map/ppermute | solution.py:21
  30.3 1.4 %collective-permute-start.3 = (bf16[2,6,1,4,258]{4,2,1,3,0:T(2,128)(2,1)S(1)}, bf16[2,6,1,4,258]{4,2,1,3,0:T(2,128)(2,1)S(1)}, u32[]{:S(2)}, u32[]{:S(2)}) collective-permute-start(bf16[2,6,1,4,258]{4,2,1,3,0:T(2,128)(2,1)S(1)} %get-tuple-element.99), channel_id=1, source_target_pairs={{1,0},{2,1},{3,2},{0,3},{5,4},{6,5},{7,6},{4,7},{9,8},{10,9},{11,1... | collective-permute-start | bytes 74312 | tf_op jit(solution)/shard_map/ppermute | solution.py:22
  32.2 0.6 copy-done.11
  32.9 0.6 dynamic-slice.44
  34.1 0.5 collective-permute-done.2
  34.6 1.3 %collective-permute-done.3 = bf16[2,6,1,4,258]{4,2,1,3,0:T(2,128)(2,1)S(1)} collective-permute-done((bf16[2,6,1,4,258]{4,2,1,3,0:T(2,128)(2,1)S(1)}, bf16[2,6,1,4,258]{4,2,1,3,0:T(2,128)(2,1)S(1)}, u32[]{:S(2)}, u32[]{:S(2)}) %collective-permute-start.3) | collective-permute-done | bytes 24800 | tf_op jit(solution)/shard_map/ppermute | solution.py:22
  35.9 0.4 maximum_convert_fusion
  36.3 0.4 fusion.3
  36.7 0.4 copy-done.5
  37.1 0.2 fusion.40
  37.5 0.2 copy.181
  37.7 1.1 convolution_bitcast_fusion
  38.8 0.9 copy.183
  39.8 0.2 copy.156
  40.0 1.1 convolution_bitcast_fusion.1
  41.1 0.9 copy.158
  42.0 0.8 copy-done.3
  42.8 0.2 fusion.43
  43.0 51.3 %all-reduce.9.cloned.1.call-done = (f32[16,6,2,128]{3,2,1,0:T(2,128)}, f32[16,6,2,128]{3,2,1,0:T(2,128)}) async-done(((f32[16,6,2,128]{3,2,1,0:T(2,128)}, f32[16,6,2,128]{3,2,1,0:T(2,128)}), (f32[16,6,2,128]{3,2,1,0:T(2,128)}, f32[16,6,2,128]{3,2,1,0:T(2,128)})) %all-reduce.9.cloned.1.call-update) | async-done | bytes 196624
  94.3 0.7 fusion.50
  95.4 3.5 %collective-permute-start.5 = (bf16[2,6,2,4,1]{4,2,1,3,0:T(2,128)(2,1)S(1)}, bf16[2,6,2,4,1]{4,2,1,3,0:T(2,128)(2,1)S(1)}, u32[]{:S(2)}, u32[]{:S(2)}) collective-permute-start(bf16[2,6,2,4,1]{4,2,1,3,0:T(2,128)(2,1)S(1)} %get-tuple-element.113), channel_id=1, source_target_pairs={{4,0},{8,4},{12,8},{16,12},{20,16},{24,20},{28,24},{0,28},{5,1},{9... | collective-permute-start | bytes 584 | tf_op jit(solution)/shard_map/ppermute | solution.py:22
  99.0 1.6 %collective-permute-done.4 = bf16[2,6,2,4,1]{4,2,1,3,0:T(2,128)(2,1)S(1)} collective-permute-done((bf16[2,6,2,4,1]{4,2,1,3,0:T(2,128)(2,1)S(1)}, bf16[2,6,2,4,1]{4,2,1,3,0:T(2,128)(2,1)S(1)}, u32[]{:S(2)}, u32[]{:S(2)}) %collective-permute-start.4) | collective-permute-done | bytes 224 | tf_op jit(solution)/shard_map/ppermute | solution.py:21
  100.6 0.2 pad_maximum_fusion.3
  100.8 0.1 fusion.59
  100.9 1.5 %collective-permute-start.6 = (bf16[2,6,1,4,258]{4,2,1,3,0:T(2,128)(2,1)S(1)}, bf16[2,6,1,4,258]{4,2,1,3,0:T(2,128)(2,1)S(1)}, u32[]{:S(2)}, u32[]{:S(2)}) collective-permute-start(bf16[2,6,1,4,258]{4,2,1,3,0:T(2,128)(2,1)S(1)} %get-tuple-element.96), channel_id=1, source_target_pairs={{0,1},{1,2},{2,3},{3,0},{4,5},{5,6},{6,7},{7,4},{8,9},{9,10},{10,1... | collective-permute-start | bytes 74312 | tf_op jit(solution)/shard_map/ppermute | solution.py:21
  102.5 1.5 %collective-permute-start.7 = (bf16[2,6,1,4,258]{4,2,1,3,0:T(2,128)(2,1)S(1)}, bf16[2,6,1,4,258]{4,2,1,3,0:T(2,128)(2,1)S(1)}, u32[]{:S(2)}, u32[]{:S(2)}) collective-permute-start(bf16[2,6,1,4,258]{4,2,1,3,0:T(2,128)(2,1)S(1)} %get-tuple-element.97), channel_id=1, source_target_pairs={{1,0},{2,1},{3,2},{0,3},{5,4},{6,5},{7,6},{4,7},{9,8},{10,9},{11,1... | collective-permute-start | bytes 74312 | tf_op jit(solution)/shard_map/ppermute | solution.py:22
  103.9 0.7 fusion.49
  104.7 1.6 %collective-permute-done.6 = bf16[2,6,1,4,258]{4,2,1,3,0:T(2,128)(2,1)S(1)} collective-permute-done((bf16[2,6,1,4,258]{4,2,1,3,0:T(2,128)(2,1)S(1)}, bf16[2,6,1,4,258]{4,2,1,3,0:T(2,128)(2,1)S(1)}, u32[]{:S(2)}, u32[]{:S(2)}) %collective-permute-start.6) | collective-permute-done | bytes 24800 | tf_op jit(solution)/shard_map/ppermute | solution.py:21
  106.2 0.8 collective-permute-done.7
  107.0 0.4 maximum_convert_fusion.1
  107.4 0.4 fusion.7
  107.8 0.2 fusion.34
  108.0 0.6 copy.188
  108.7 0.2 fusion.37
  108.9 0.6 copy.187
  (80 shorter events, 1.9 us)
Async XLA Ops:
  7.2 6.6 %copy-start = (s32[2,16,4]{1,2,0:T(4,128)S(1)}, s32[2,16,4]{1,2,0:T(4,128)}, u32[]{:S(2)}) copy-start(s32[2,16,4]{1,2,0:T(4,128)} %param.33) | copy-start | bytes 1540
  7.2 87.1 %all-reduce.9.cloned.1.call-start = ((), (), s32[]{:S(2)}) async-start(), calls=%async_computation | async-start | bytes 393216
  8.1 4.8 %copy-start.7 = (bf16[6,6,2,4,256]{4,3,2,1,0:T(4,128)(2,1)S(1)}, bf16[6,6,2,4,256]{4,3,2,1,0:T(4,128)(2,1)}, u32[]{:S(2)}) copy-start(bf16[6,6,2,4,256]{4,3,2,1,0:T(4,128)(2,1)} %param.29) | copy-start | bytes 442372
  8.2 4.7 %copy-start.2 = (f32[6,2,4,256]{3,2,1,0:T(4,128)S(1)}, f32[6,2,4,256]{3,2,1,0:T(4,128)}, u32[]{:S(2)}) copy-start(f32[6,2,4,256]{3,2,1,0:T(4,128)} %param.25) | copy-start | bytes 147460
  8.3 20.1 %collective-permute-start = (bf16[2,6,2,4,1]{4,2,1,3,0:T(2,128)(2,1)S(1)}, bf16[2,6,2,4,1]{4,2,1,3,0:T(2,128)(2,1)S(1)}, u32[]{:S(2)}, u32[]{:S(2)}) collective-permute-start(bf16[2,6,2,4,1]{4,2,1,3,0:T(2,128)(2,1)S(1)} %get-tuple-element.128), channel_id=1, source_target_pairs={{0,4},{4,8},{8,12},{12,16},{16,20},{20,24},{24,28},{28,0},{1,5},{5... | collective-permute-start | bytes 584 | tf_op jit(solution)/shard_map/ppermute | solution.py:21
  8.8 19.6 %collective-permute-start.1 = (bf16[2,6,2,4,1]{4,2,1,3,0:T(2,128)(2,1)S(1)}, bf16[2,6,2,4,1]{4,2,1,3,0:T(2,128)(2,1)S(1)}, u32[]{:S(2)}, u32[]{:S(2)}) collective-permute-start(bf16[2,6,2,4,1]{4,2,1,3,0:T(2,128)(2,1)S(1)} %get-tuple-element.129), channel_id=1, source_target_pairs={{4,0},{8,4},{12,8},{16,12},{20,16},{24,20},{28,24},{0,28},{5,1},{9... | collective-permute-start | bytes 584 | tf_op jit(solution)/shard_map/ppermute | solution.py:22
  13.0 0.7 copy-start.10
  14.9 0.7 copy-start.9
  26.4 0.9 copy-start.8
  27.4 1.0 copy-start.1
  28.8 5.8 %collective-permute-start.2 = (bf16[2,6,1,4,258]{4,2,1,3,0:T(2,128)(2,1)S(1)}, bf16[2,6,1,4,258]{4,2,1,3,0:T(2,128)(2,1)S(1)}, u32[]{:S(2)}, u32[]{:S(2)}) collective-permute-start(bf16[2,6,1,4,258]{4,2,1,3,0:T(2,128)(2,1)S(1)} %get-tuple-element.98), channel_id=1, source_target_pairs={{0,1},{1,2},{2,3},{3,0},{4,5},{5,6},{6,7},{7,4},{8,9},{9,10},{10,1... | collective-permute-start | bytes 74312 | tf_op jit(solution)/shard_map/ppermute | solution.py:21
  30.3 5.6 %collective-permute-start.3 = (bf16[2,6,1,4,258]{4,2,1,3,0:T(2,128)(2,1)S(1)}, bf16[2,6,1,4,258]{4,2,1,3,0:T(2,128)(2,1)S(1)}, u32[]{:S(2)}, u32[]{:S(2)}) collective-permute-start(bf16[2,6,1,4,258]{4,2,1,3,0:T(2,128)(2,1)S(1)} %get-tuple-element.99), channel_id=1, source_target_pairs={{1,0},{2,1},{3,2},{0,3},{5,4},{6,5},{7,6},{4,7},{9,8},{10,9},{11,1... | collective-permute-start | bytes 74312 | tf_op jit(solution)/shard_map/ppermute | solution.py:22
  32.2 0.7 copy-start.11
  36.2 0.8 copy-start.5
  36.3 0.8 copy-start.6
  42.0 0.8 copy-start.3
  42.0 0.8 copy-start.4
  95.3 5.3 %collective-permute-start.4 = (bf16[2,6,2,4,1]{4,2,1,3,0:T(2,128)(2,1)S(1)}, bf16[2,6,2,4,1]{4,2,1,3,0:T(2,128)(2,1)S(1)}, u32[]{:S(2)}, u32[]{:S(2)}) collective-permute-start(bf16[2,6,2,4,1]{4,2,1,3,0:T(2,128)(2,1)S(1)} %get-tuple-element.112), channel_id=1, source_target_pairs={{0,4},{4,8},{8,12},{12,16},{16,20},{20,24},{24,28},{28,0},{1,5},{5... | collective-permute-start | bytes 584 | tf_op jit(solution)/shard_map/ppermute | solution.py:21
  95.4 5.2 %collective-permute-start.5 = (bf16[2,6,2,4,1]{4,2,1,3,0:T(2,128)(2,1)S(1)}, bf16[2,6,2,4,1]{4,2,1,3,0:T(2,128)(2,1)S(1)}, u32[]{:S(2)}, u32[]{:S(2)}) collective-permute-start(bf16[2,6,2,4,1]{4,2,1,3,0:T(2,128)(2,1)S(1)} %get-tuple-element.113), channel_id=1, source_target_pairs={{4,0},{8,4},{12,8},{16,12},{20,16},{24,20},{28,24},{0,28},{5,1},{9... | collective-permute-start | bytes 584 | tf_op jit(solution)/shard_map/ppermute | solution.py:22
  100.9 5.3 %collective-permute-start.6 = (bf16[2,6,1,4,258]{4,2,1,3,0:T(2,128)(2,1)S(1)}, bf16[2,6,1,4,258]{4,2,1,3,0:T(2,128)(2,1)S(1)}, u32[]{:S(2)}, u32[]{:S(2)}) collective-permute-start(bf16[2,6,1,4,258]{4,2,1,3,0:T(2,128)(2,1)S(1)} %get-tuple-element.96), channel_id=1, source_target_pairs={{0,1},{1,2},{2,3},{3,0},{4,5},{5,6},{6,7},{7,4},{8,9},{9,10},{10,1... | collective-permute-start | bytes 74312 | tf_op jit(solution)/shard_map/ppermute | solution.py:21
  102.5 4.6 %collective-permute-start.7 = (bf16[2,6,1,4,258]{4,2,1,3,0:T(2,128)(2,1)S(1)}, bf16[2,6,1,4,258]{4,2,1,3,0:T(2,128)(2,1)S(1)}, u32[]{:S(2)}, u32[]{:S(2)}) collective-permute-start(bf16[2,6,1,4,258]{4,2,1,3,0:T(2,128)(2,1)S(1)} %get-tuple-element.97), channel_id=1, source_target_pairs={{1,0},{2,1},{3,2},{0,3},{5,4},{6,5},{7,6},{4,7},{9,8},{10,9},{11,1... | collective-permute-start | bytes 74312 | tf_op jit(solution)/shard_map/ppermute | solution.py:22
Sparse Core Ops, SparseCore 0:
  42.2 52.1 all-reduce.8
where the time goes:
time: 117 us; the launch traced here: 116 us
  waiting for transfers between devices  57.1 us (49%)
  between operations  15.2 us (13%)
  starting transfers between devices  14.2 us (12%)
  blocking collectives  10.8 us (9%)
  local copies, waits for them, and re-layouts  10.3 us (9%)
  other arithmetic  4.62 us (4%)
  matrix products  4.18 us (4%)
    unnamed x2, waiting for transfers between devices  51.3 us
    all_gather x1, blocking collectives, per_device(): portion = lax.all_gather(rotor_state, 'circ', axis=2, tiled=True)  10.8 us
    ppermute x4, starting transfers between devices, extended(): after = lax.ppermute(first, axis, down)  10.5 us
    unnamed x29, local copies, waits for them, and re-layouts  5.55 us
    ppermute x4, waiting for transfers between devices, extended(): before = lax.ppermute(last, axis, up)  3.7 us
    ppermute x4, starting transfers between devices, extended(): before = lax.ppermute(last, axis, up)  3.62 us
  transfers between devices with their start and end apart: 9, of which 6 were waited for; matrix products, arithmetic and copies ran while one was open for 4% of the time, Pallas kernels for 0%

commit v1 on v0

--- a/solution.py
+++ b/solution.py
@@ -86,6 +86,11 @@
         .at[span_rows - 1]
         .set(high_keep)[None, None, :, None, None]
     )
+    reached = first_block + jnp.arange(own_blocks, dtype=jnp.int32)
+    pull_one_hot = (
+        margin_block[:, None, :, :] == reached[None, :, None, None]
+    ).astype(jnp.float32)
+    pull_mixing = jnp.einsum("sjbk,sbkc->sjbc", pull_one_hot, weights_live, precision=highest)
     rotor_adj, stator_adj = (adjoint_rotor, adjoint_stator)
     for sweep in range(STEPS):
         stacked = jnp.stack((rotor_adj, stator_adj))
@@ -106,20 +111,13 @@
         flux_blocks = flux_wire.astype(jnp.float32).reshape(
             var_count, span_rows, own_blocks, block_width
         )
-        one_hot = (
-            own_ids[:, :, :, None]
-            == jnp.arange(own_blocks * lax.axis_size("circ"), dtype=jnp.int32)[None, None, None, :]
-        ).astype(jnp.float32)
-        mixing = jnp.einsum("sbkj,sbkc->sbjc", one_hot, own_weights, precision=highest)
-        pulled_blocks = lax.psum_scatter(
-            jnp.einsum("sbjc,vsbc->jvsc", mixing, flux_blocks, precision=highest),
-            "circ",
-            scatter_dimension=0,
-            tiled=True,
+        gathered = lax.all_gather(flux_wire, "circ", axis=2, tiled=True)
+        gathered_blocks = gathered.astype(jnp.float32).reshape(
+            var_count, span_rows, row_count, block_width
         )
-        pulled = jnp.transpose(pulled_blocks, (1, 2, 0, 3)).reshape(
-            var_count, span_rows, cell_count
-        )
+        pulled = jnp.einsum(
+            "sjbc,vsbc->vsjc", pull_mixing, gathered_blocks, precision=highest
+        ).reshape(var_count, span_rows, cell_count)
         rotor_res = (
             jacobian_apply(jac_diag_rotor, jac_off_rotor, rotor_adj)
             - coupling * beside_all[0]

time: 117 us -> 65.6 us (0.56)
  waiting for transfers between devices: 57.1 us -> 3.94 us
  blocking collectives: 10.8 us -> 28.3 us
  between operations: 15.2 us -> 1.2 us
    unnamed x2 -> x0, waiting for transfers between devices: 51.3 us -> none
    all_gather x0 -> x2, blocking collectives: none -> 17.5 us  [per_device(): gathered = lax.all_gather(flux_wire, 'circ', axis=2, tiled=True)]
    transpose x2, local copies, waits for them, and re-layouts: 1.86 us -> 0.26 us  [the longest x1 0.16 us: per_device(): jnp.einsum('sjbk,sbkc->sjbc', pull_one_hot, weights_live, precision=highest)]
    neg x2 -> x0, other arithmetic: 1.42 us -> none  [per_device(): rotor_res = rotor_res.at[:, :, layer_count - 1, :].add(-pulled)]
  transfers between devices with their start and end apart: 9 -> 8, of which waited for: 6 -> 2; matrix products, arithmetic and copies ran while one was open for 4% -> 5% of each run, Pallas kernels for 0% -> 0%
where the time goes in v1:
time: 65.6 us; the launch traced here: 65.1 us
  blocking collectives  28.3 us (43%)
  starting transfers between devices  14.2 us (22%)
  local copies, waits for them, and re-layouts  9.98 us (15%)
  waiting for transfers between devices  3.94 us (6%)
  matrix products  3.89 us (6%)
  other arithmetic  3.62 us (6%)
  between operations  1.2 us (2%)
    all_gather x2, blocking collectives, per_device(): gathered = lax.all_gather(flux_wire, 'circ', axis=2, tiled=True)  17.5 us
    all_gather x1, blocking collectives, per_device(): portion = lax.all_gather(rotor_state, 'circ', axis=2, tiled=True)  10.8 us
    ppermute x4, starting transfers between devices, extended(): after = lax.ppermute(first, axis, down)  10.7 us
    unnamed x29, local copies, waits for them, and re-layouts  5.81 us
    ppermute x4, starting transfers between devices, extended(): before = lax.ppermute(last, axis, up)  3.52 us
    ppermute x4, waiting for transfers between devices, extended(): before = lax.ppermute(last, axis, up)  2.86 us
    dot_general x2, matrix products, per_device(): jnp.einsum('sjbc,vsbc->vsjc', pull_mixing, gathered_blocks, precision=hig...  1.94 us
    dot_general x1, matrix products, per_device(): jnp.einsum('sbjc,vsjc->vsbc', pick_mixing, blocks, precision=highest)  1.35 us
  transfers between devices with their start and end apart: 8, of which 2 were waited for; matrix products, arithmetic and copies ran while one was open for 5% of the time, Pallas kernels for 0%

profile of v1, /device:TPU:0, one launch (start us, length us, event | category | flops | bytes accessed | tf_op | source)
XLA Modules:
  0.0 65.1 jit_solution(14401710043318745020)
XLA Ops:
  0.6 0.9 %copy_bitcast_fusion = (f32[1,6,2,4,256]{4,2,1,3,0:T(2,128)S(1)}, f32[1,6,2,4,256]{4,2,1,3,0:T(2,128)S(1)}) fusion(f32[6,2,4,256]{3,2,1,0:T(4,128)} %param.24, f32[6,2,4,256]{3,2,1,0:T(4,128)} %param.25), kind=kLoop, calls=%fused_computation.103 | loop fusion | bytes 196608 | tf_op jit(solution)/shard_map/stack | solution.py:96
  1.7 0.5 collective-permute-start
  2.2 4.1 %collective-permute-start.1 = (bf16[2,6,2,4,1]{4,2,1,3,0:T(2,128)(2,1)S(1)}, bf16[2,6,2,4,1]{4,2,1,3,0:T(2,128)(2,1)S(1)}, u32[]{:S(2)}, u32[]{:S(2)}) collective-permute-start(bf16[2,6,2,4,1]{4,2,1,3,0:T(2,128)(2,1)S(1)} %get-tuple-element.129), channel_id=1, source_target_pairs={{4,0},{8,4},{12,8},{16,12},{20,16},{24,20},{28,24},{0,28},{5,1},{9... | collective-permute-start | bytes 584 | tf_op jit(solution)/shard_map/ppermute | solution.py:22
  6.3 0.8 %copy-done = f32[6,2,4,256]{3,2,1,0:T(4,128)S(1)} copy-done((f32[6,2,4,256]{3,2,1,0:T(4,128)S(1)}, f32[6,2,4,256]{3,2,1,0:T(4,128)}, u32[]{:S(2)}) %copy-start) | copy-done | bytes 49176
  7.2 0.7 %copy-done.9 = s32[2,16,4]{1,2,0:T(4,128)S(1)} copy-done((s32[2,16,4]{1,2,0:T(4,128)S(1)}, s32[2,16,4]{1,2,0:T(4,128)}, u32[]{:S(2)}) %copy-start.9) | copy-done | bytes 536
  8.1 0.6 copy-done.11
  8.9 0.8 %copy-done.8 = f32[2,16,4,128]{3,2,1,0:T(4,128)S(1)} copy-done((f32[2,16,4,128]{3,2,1,0:T(4,128)S(1)}, f32[2,16,4,128]{3,2,1,0:T(4,128)}, u32[]{:S(2)}) %copy-start.8) | copy-done | bytes 65560
  9.7 0.3 convolution_bitcast_fusion.1
  10.1 0.3 fusion.58
  10.4 0.2 pad_maximum_fusion.2
  10.6 0.1 fusion.67
  10.7 2.0 %collective-permute-start.2 = (bf16[2,6,1,4,258]{4,2,1,3,0:T(2,128)(2,1)S(1)}, bf16[2,6,1,4,258]{4,2,1,3,0:T(2,128)(2,1)S(1)}, u32[]{:S(2)}, u32[]{:S(2)}) collective-permute-start(bf16[2,6,1,4,258]{4,2,1,3,0:T(2,128)(2,1)S(1)} %get-tuple-element.98), channel_id=1, source_target_pairs={{0,1},{1,2},{2,3},{3,0},{4,5},{5,6},{6,7},{7,4},{8,9},{9,10},{10,1... | collective-permute-start | bytes 74312 | tf_op jit(solution)/shard_map/ppermute | solution.py:21
  12.7 1.0 %collective-permute-start.3 = (bf16[2,6,1,4,258]{4,2,1,3,0:T(2,128)(2,1)S(1)}, bf16[2,6,1,4,258]{4,2,1,3,0:T(2,128)(2,1)S(1)}, u32[]{:S(2)}, u32[]{:S(2)}) collective-permute-start(bf16[2,6,1,4,258]{4,2,1,3,0:T(2,128)(2,1)S(1)} %get-tuple-element.99), channel_id=1, source_target_pairs={{1,0},{2,1},{3,2},{0,3},{5,4},{6,5},{7,6},{4,7},{9,8},{10,9},{11,1... | collective-permute-start | bytes 74312 | tf_op jit(solution)/shard_map/ppermute | solution.py:22
  13.9 0.2 copy.202
  14.1 0.5 copy-done.10
  14.6 10.8 %all_gather.9 = bf16[6,2,2048]{2,1,0:T(2,128)(2,1)S(1)} all-gather(bf16[6,2,256]{2,1,0:T(2,128)(2,1)S(1)} %copy-done.10), channel_id=1, replica_groups=mesh['circ'=8,'span'=4] {'circ'}, dimensions={2}, use_global_device_ids=true | all-gather | bytes 55296 | tf_op jit(solution)/shard_map/all_gather | solution.py:71
  25.4 0.3 copy.203
  25.7 0.2 copy.211
  26.0 0.4 maximum_convert_fusion
  26.4 0.4 fusion.5
  26.8 0.4 copy-done.4
  27.2 0.2 fusion.43
  27.4 0.2 copy.206
  27.6 1.4 %multiply_reduce_fusion.1 = (f32[2,2,128]{1,2,0:T(8,128)S(1)}, f32[2,2,128]{1,2,0:T(8,128)S(1)}, f32[6,2,2,128]{0,2,3,1:T(2,128)S(1)}) fusion(f32[6,2,2,128]{0,2,3,1:T(2,128)S(1)} %copy.206, f32[2,2,16,128]{2,1,3,0:T(2,128)S(1)} %copy.202, bf16[6,2,16,128]{2,0,3,1:T(8,128)(2,1)S(1)} %copy.203), kind=kOutput, calls=%fused_computation.7 | convolution fusion | flops 601088 | bytes 110592 | tf_op jit(solution)/shard_map/sbjc,vsjc->vsbc/dot_general | solution.py:78
  29.5 0.2 copy.233
  29.6 0.4 multiply_reduce_fusion
  30.2 8.9 %all_gather.10 = bf16[6,2,2048]{2,1,0:T(2,128)(2,1)S(1)} all-gather(bf16[6,2,256]{2,1,0:T(2,128)(2,1)S(1)} %get-tuple-element.131), channel_id=1, replica_groups=mesh['circ'=8,'span'=4] {'circ'}, dimensions={2}, use_global_device_ids=true | all-gather | bytes 55296 | tf_op jit(solution)/shard_map/all_gather | solution.py:114
  39.1 0.3 copy.210
  39.4 1.0 %fusion.1 = f32[6,2,2,128]{0,2,3,1:T(2,128)S(1)} fusion(bf16[6,2,16,128]{2,0,3,1:T(8,128)(2,1)S(1)} %copy.210, f32[2,2,16,128]{2,1,3,0:T(2,128)S(1)} %copy.211), kind=kOutput, calls=%fused_computation.3 | convolution fusion | flops 592896 | bytes 94208 | tf_op jit(solution)/shard_map/sjbc,vsbc->vsjc/dot_general | solution.py:118
  40.6 0.6 copy-done.2
  41.2 0.2 fusion.46
  41.6 0.4 collective-permute-start.4
  42.0 3.2 %collective-permute-start.5 = (bf16[2,6,2,4,1]{4,2,1,3,0:T(2,128)(2,1)S(1)}, bf16[2,6,2,4,1]{4,2,1,3,0:T(2,128)(2,1)S(1)}, u32[]{:S(2)}, u32[]{:S(2)}) collective-permute-start(bf16[2,6,2,4,1]{4,2,1,3,0:T(2,128)(2,1)S(1)} %get-tuple-element.113), channel_id=1, source_target_pairs={{4,0},{8,4},{12,8},{16,12},{20,16},{24,20},{28,24},{0,28},{5,1},{9... | collective-permute-start | bytes 584 | tf_op jit(solution)/shard_map/ppermute | solution.py:22
  45.2 8.6 %all_gather.11 = bf16[6,2,2048]{2,1,0:T(2,128)(2,1)S(1)} all-gather(bf16[6,2,256]{2,1,0:T(2,128)(2,1)S(1)} %get-tuple-element.130), channel_id=1, replica_groups=mesh['circ'=8,'span'=4] {'circ'}, dimensions={2}, use_global_device_ids=true | all-gather | bytes 55296 | tf_op jit(solution)/shard_map/all_gather | solution.py:114
  53.9 0.3 copy.235
  54.2 1.0 %fusion = f32[6,2,2,128]{0,2,3,1:T(2,128)S(1)} fusion(bf16[6,2,16,128]{2,0,3,1:T(8,128)(2,1)S(1)} %copy.235, f32[2,2,16,128]{2,1,3,0:T(2,128)S(1)} %copy.211), kind=kOutput, calls=%fused_computation.1 | convolution fusion | flops 592896 | bytes 94208 | tf_op jit(solution)/shard_map/sjbc,vsbc->vsjc/dot_general | solution.py:118
  55.2 0.2 pad_maximum_fusion.3
  55.4 0.1 fusion.66
  55.5 0.6 collective-permute-start.6
  56.2 2.3 %collective-permute-start.7 = (bf16[2,6,1,4,258]{4,2,1,3,0:T(2,128)(2,1)S(1)}, bf16[2,6,1,4,258]{4,2,1,3,0:T(2,128)(2,1)S(1)}, u32[]{:S(2)}, u32[]{:S(2)}) collective-permute-start(bf16[2,6,1,4,258]{4,2,1,3,0:T(2,128)(2,1)S(1)} %get-tuple-element.97), channel_id=1, source_target_pairs={{1,0},{2,1},{3,2},{0,3},{5,4},{6,5},{7,6},{4,7},{9,8},{10,9},{11,1... | collective-permute-start | bytes 74312 | tf_op jit(solution)/shard_map/ppermute | solution.py:22
  58.7 2.9 %collective-permute-done.6 = bf16[2,6,1,4,258]{4,2,1,3,0:T(2,128)(2,1)S(1)} collective-permute-done((bf16[2,6,1,4,258]{4,2,1,3,0:T(2,128)(2,1)S(1)}, bf16[2,6,1,4,258]{4,2,1,3,0:T(2,128)(2,1)S(1)}, u32[]{:S(2)}, u32[]{:S(2)}) %collective-permute-start.6) | collective-permute-done | bytes 24800 | tf_op jit(solution)/shard_map/ppermute | solution.py:21
  61.5 1.1 %collective-permute-done.7 = bf16[2,6,1,4,258]{4,2,1,3,0:T(2,128)(2,1)S(1)} collective-permute-done((bf16[2,6,1,4,258]{4,2,1,3,0:T(2,128)(2,1)S(1)}, bf16[2,6,1,4,258]{4,2,1,3,0:T(2,128)(2,1)S(1)}, u32[]{:S(2)}, u32[]{:S(2)}) %collective-permute-start.7) | collective-permute-done | bytes 24800 | tf_op jit(solution)/shard_map/ppermute | solution.py:22
  62.6 0.4 maximum_convert_fusion.1
  63.0 0.4 fusion.9
  63.4 0.2 fusion.37
  63.6 0.6 copy.241
  64.3 0.2 fusion.40
  64.5 0.6 copy.240
  (85 shorter events, 2.4 us)
Async XLA Ops:
  1.5 5.6 %copy-start.6 = (bf16[6,6,2,4,256]{4,3,2,1,0:T(4,128)(2,1)S(1)}, bf16[6,6,2,4,256]{4,3,2,1,0:T(4,128)(2,1)}, u32[]{:S(2)}) copy-start(bf16[6,6,2,4,256]{4,3,2,1,0:T(4,128)(2,1)} %param.29) | copy-start | bytes 442372
  1.6 4.7 %copy-start.1 = (f32[6,2,4,256]{3,2,1,0:T(4,128)S(1)}, f32[6,2,4,256]{3,2,1,0:T(4,128)}, u32[]{:S(2)}) copy-start(f32[6,2,4,256]{3,2,1,0:T(4,128)} %param.25) | copy-start | bytes 147460
  1.7 8.7 %collective-permute-start = (bf16[2,6,2,4,1]{4,2,1,3,0:T(2,128)(2,1)S(1)}, bf16[2,6,2,4,1]{4,2,1,3,0:T(2,128)(2,1)S(1)}, u32[]{:S(2)}, u32[]{:S(2)}) collective-permute-start(bf16[2,6,2,4,1]{4,2,1,3,0:T(2,128)(2,1)S(1)} %get-tuple-element.128), channel_id=1, source_target_pairs={{0,4},{4,8},{8,12},{12,16},{16,20},{20,24},{24,28},{28,0},{1,5},{5... | collective-permute-start | bytes 584 | tf_op jit(solution)/shard_map/ppermute | solution.py:21
  2.2 8.2 %collective-permute-start.1 = (bf16[2,6,2,4,1]{4,2,1,3,0:T(2,128)(2,1)S(1)}, bf16[2,6,2,4,1]{4,2,1,3,0:T(2,128)(2,1)S(1)}, u32[]{:S(2)}, u32[]{:S(2)}) collective-permute-start(bf16[2,6,2,4,1]{4,2,1,3,0:T(2,128)(2,1)S(1)} %get-tuple-element.129), channel_id=1, source_target_pairs={{4,0},{8,4},{12,8},{16,12},{20,16},{24,20},{28,24},{0,28},{5,1},{9... | collective-permute-start | bytes 584 | tf_op jit(solution)/shard_map/ppermute | solution.py:22
  6.3 0.8 %copy-start = (f32[6,2,4,256]{3,2,1,0:T(4,128)S(1)}, f32[6,2,4,256]{3,2,1,0:T(4,128)}, u32[]{:S(2)}) copy-start(f32[6,2,4,256]{3,2,1,0:T(4,128)} %param.24) | copy-start | bytes 147460
  7.1 1.7 %copy-start.7 = (bf16[6,6,2,4,256]{4,3,2,1,0:T(4,128)(2,1)S(1)}, bf16[6,6,2,4,256]{4,3,2,1,0:T(4,128)(2,1)}, u32[]{:S(2)}) copy-start(bf16[6,6,2,4,256]{4,3,2,1,0:T(4,128)(2,1)} %param.28) | copy-start | bytes 442372
  7.2 0.7 %copy-start.9 = (s32[2,16,4]{1,2,0:T(4,128)S(1)}, s32[2,16,4]{1,2,0:T(4,128)}, u32[]{:S(2)}) copy-start(s32[2,16,4]{1,2,0:T(4,128)} %param.33) | copy-start | bytes 1540
  8.0 0.7 %copy-start.11 = (s32[2,16]{1,0:T(2,128)S(1)}, s32[2,16]{1,0:T(2,128)}, u32[]{:S(2)}) copy-start(s32[2,16]{1,0:T(2,128)} %param.34) | copy-start | bytes 388
  8.8 0.8 %copy-start.8 = (f32[2,16,4,128]{3,2,1,0:T(4,128)S(1)}, f32[2,16,4,128]{3,2,1,0:T(4,128)}, u32[]{:S(2)}) copy-start(f32[2,16,4,128]{3,2,1,0:T(4,128)} %param.35) | copy-start | bytes 196612
  10.7 15.3 %collective-permute-start.2 = (bf16[2,6,1,4,258]{4,2,1,3,0:T(2,128)(2,1)S(1)}, bf16[2,6,1,4,258]{4,2,1,3,0:T(2,128)(2,1)S(1)}, u32[]{:S(2)}, u32[]{:S(2)}) collective-permute-start(bf16[2,6,1,4,258]{4,2,1,3,0:T(2,128)(2,1)S(1)} %get-tuple-element.98), channel_id=1, source_target_pairs={{0,1},{1,2},{2,3},{3,0},{4,5},{5,6},{6,7},{7,4},{8,9},{9,10},{10,1... | collective-permute-start | bytes 74312 | tf_op jit(solution)/shard_map/ppermute | solution.py:21
  12.7 13.3 %collective-permute-start.3 = (bf16[2,6,1,4,258]{4,2,1,3,0:T(2,128)(2,1)S(1)}, bf16[2,6,1,4,258]{4,2,1,3,0:T(2,128)(2,1)S(1)}, u32[]{:S(2)}, u32[]{:S(2)}) collective-permute-start(bf16[2,6,1,4,258]{4,2,1,3,0:T(2,128)(2,1)S(1)} %get-tuple-element.99), channel_id=1, source_target_pairs={{1,0},{2,1},{3,2},{0,3},{5,4},{6,5},{7,6},{4,7},{9,8},{10,9},{11,1... | collective-permute-start | bytes 74312 | tf_op jit(solution)/shard_map/ppermute | solution.py:22
  13.9 0.7 %copy-start.10 = (bf16[6,2,256]{2,1,0:T(2,128)(2,1)S(1)}, bf16[6,2,256]{2,1,0:T(2,128)(2,1)}, u32[]{:S(2)}) copy-start(bf16[6,2,256]{2,1,0:T(2,128)(2,1)} %param.32) | copy-start | bytes 18436
  26.4 0.8 %copy-start.4 = (f32[6,2,4,256]{3,2,1,0:T(4,128)S(1)}, f32[6,2,4,256]{3,2,1,0:T(4,128)}, u32[]{:S(2)}) copy-start(f32[6,2,4,256]{3,2,1,0:T(4,128)} %param.31) | copy-start | bytes 147460
  26.4 0.8 %copy-start.5 = (f32[6,2,4,256]{3,2,1,0:T(4,128)S(1)}, f32[6,2,4,256]{3,2,1,0:T(4,128)}, u32[]{:S(2)}) copy-start(f32[6,2,4,256]{3,2,1,0:T(4,128)} %param.27) | copy-start | bytes 147460
  40.4 0.8 %copy-start.2 = (f32[6,2,4,256]{3,2,1,0:T(4,128)S(1)}, f32[6,2,4,256]{3,2,1,0:T(4,128)}, u32[]{:S(2)}) copy-start(f32[6,2,4,256]{3,2,1,0:T(4,128)} %param.30) | copy-start | bytes 147460
  40.4 0.8 %copy-start.3 = (f32[6,2,4,256]{3,2,1,0:T(4,128)S(1)}, f32[6,2,4,256]{3,2,1,0:T(4,128)}, u32[]{:S(2)}) copy-start(f32[6,2,4,256]{3,2,1,0:T(4,128)} %param.26) | copy-start | bytes 147460
  41.6 13.6 %collective-permute-start.4 = (bf16[2,6,2,4,1]{4,2,1,3,0:T(2,128)(2,1)S(1)}, bf16[2,6,2,4,1]{4,2,1,3,0:T(2,128)(2,1)S(1)}, u32[]{:S(2)}, u32[]{:S(2)}) collective-permute-start(bf16[2,6,2,4,1]{4,2,1,3,0:T(2,128)(2,1)S(1)} %get-tuple-element.112), channel_id=1, source_target_pairs={{0,4},{4,8},{8,12},{12,16},{16,20},{20,24},{24,28},{28,0},{1,5},{5... | collective-permute-start | bytes 584 | tf_op jit(solution)/shard_map/ppermute | solution.py:21
  42.0 13.2 %collective-permute-start.5 = (bf16[2,6,2,4,1]{4,2,1,3,0:T(2,128)(2,1)S(1)}, bf16[2,6,2,4,1]{4,2,1,3,0:T(2,128)(2,1)S(1)}, u32[]{:S(2)}, u32[]{:S(2)}) collective-permute-start(bf16[2,6,2,4,1]{4,2,1,3,0:T(2,128)(2,1)S(1)} %get-tuple-element.113), channel_id=1, source_target_pairs={{4,0},{8,4},{12,8},{16,12},{20,16},{24,20},{28,24},{0,28},{5,1},{9... | collective-permute-start | bytes 584 | tf_op jit(solution)/shard_map/ppermute | solution.py:22
  55.5 6.0 %collective-permute-start.6 = (bf16[2,6,1,4,258]{4,2,1,3,0:T(2,128)(2,1)S(1)}, bf16[2,6,1,4,258]{4,2,1,3,0:T(2,128)(2,1)S(1)}, u32[]{:S(2)}, u32[]{:S(2)}) collective-permute-start(bf16[2,6,1,4,258]{4,2,1,3,0:T(2,128)(2,1)S(1)} %get-tuple-element.96), channel_id=1, source_target_pairs={{0,1},{1,2},{2,3},{3,0},{4,5},{5,6},{6,7},{7,4},{8,9},{9,10},{10,1... | collective-permute-start | bytes 74312 | tf_op jit(solution)/shard_map/ppermute | solution.py:21
  56.2 6.5 %collective-permute-start.7 = (bf16[2,6,1,4,258]{4,2,1,3,0:T(2,128)(2,1)S(1)}, bf16[2,6,1,4,258]{4,2,1,3,0:T(2,128)(2,1)S(1)}, u32[]{:S(2)}, u32[]{:S(2)}) collective-permute-start(bf16[2,6,1,4,258]{4,2,1,3,0:T(2,128)(2,1)S(1)} %get-tuple-element.97), channel_id=1, source_target_pairs={{1,0},{2,1},{3,2},{0,3},{5,4},{6,5},{7,6},{4,7},{9,8},{10,9},{11,1... | collective-permute-start | bytes 74312 | tf_op jit(solution)/shard_map/ppermute | solution.py:22
